TPU v7x, 256 devices: a whole 4x4x8 slice. The times are simulated.
256 devices in a mesh: shot: 8 (over z), rec: 32 (over y, x, core).
Axes of the slice: x: 4, y: 4, z: 8, core: 2. Of those that a mesh axis runs over, the one named last changes fastest.
Arguments:
- primaries: bfloat16 [2, 4, 2048, 4096], P(None, None, 'shot', 'rec'), may hold values from -0.0625 to 0.0625
- recorded: bfloat16 [2, 4, 4096, 4096], P(None, None, 'shot', 'rec'), may hold values from -6 to 6
Outputs:
- multiples: float32 [2, 4, 2048, 4096], P(None, None, 'shot', 'rec')
All inputs are finite; a program needn't handle non-finite values.
Results may differ from a plain program's by a relative error of at most 0.0003.
Values may be sent and summed in bfloat16 or wider, within the bound.
A program may use at most 128 MiB of HBM per device.

v0:
```python
import jax
import jax.numpy as jnp
from jax import lax
from jax.sharding import PartitionSpec as P


def complex_product(left_re, left_im, right_re, right_im):
    real_part = jnp.dot(left_re, right_re, preferred_element_type=jnp.float32) - jnp.dot(
        left_im, right_im, preferred_element_type=jnp.float32
    )
    imag_part = jnp.dot(left_re, right_im, preferred_element_type=jnp.float32) + jnp.dot(
        left_im, right_re, preferred_element_type=jnp.float32
    )
    return (real_part, imag_part)


def shards(primaries, recorded):
    real_list = []
    imag_list = []
    for frequency in range(primaries.shape[1]):
        panel = primaries[:, frequency]
        block = recorded[:, frequency]
        columns = lax.all_gather(block, "shot", axis=1, tiled=True)
        segment = lax.all_gather(panel, "rec", axis=2, tiled=True)
        real_part, imag_part = complex_product(segment[0], segment[1], columns[0], columns[1])
        real_list.append(real_part)
        imag_list.append(imag_part)
    return jnp.stack([jnp.stack(real_list, 0), jnp.stack(imag_list, 0)], 0)


def solution(mesh):
    placed = (P(None, None, "shot", "rec"), P(None, None, "shot", "rec"))
    return jax.shard_map(
        shards, mesh=mesh, in_specs=placed, out_specs=P(None, None, "shot", "rec"), check_vma=False
    )
```

profile of v0, /device:TPU:1, one launch (start us, length us, event | category | flops | bytes accessed | tf_op | source)
XLA Modules:
  0.0 426.4 jit_solution(16314969737826655694)
XLA Ops:
  6.5 2.2 fusion.32
  8.8 0.8 fusion.33
  12.2 0.7 all-gather.19.cloned.1.call-update
  12.9 0.7 all-gather.17.cloned.1.call-update
  13.6 36.8 %all-gather.27.cloned.1.call-done = bf16[2,1,4096,128]{3,2,1,0:T(8,128)(2,1)} async-done(((bf16[2,1,512,128]{3,2,1,0:T(8,128)(2,1)}), bf16[2,1,4096,128]{3,2,1,0:T(8,128)(2,1)}) %all-gather.27.cloned.1.call-update) | async-done | bytes 2097168 | tf_op jit(solution)/shard_map/all_gather | solution.py:23
  50.4 59.4 %all-gather.25.cloned.1.call-done = bf16[2,1,256,4096]{3,2,1,0:T(8,128)(2,1)} async-done(((bf16[2,1,256,128]{3,2,1,0:T(8,128)(2,1)}), bf16[2,1,256,4096]{3,2,1,0:T(8,128)(2,1)}) %all-gather.25.cloned.1.call-update) | async-done | bytes 4194320 | tf_op jit(solution)/shard_map/all_gather | solution.py:24
  109.8 2.7 fusion.8
  113.0 2.0 fusion.9
  114.9 33.3 %all-gather.31.cloned.1.call-done = bf16[2,1,4096,128]{3,2,1,0:T(8,128)(2,1)} async-done(((bf16[2,1,512,128]{3,2,1,0:T(8,128)(2,1)}), bf16[2,1,4096,128]{3,2,1,0:T(8,128)(2,1)}) %all-gather.31.cloned.1.call-update) | async-done | bytes 2097168 | tf_op jit(solution)/shard_map/all_gather | solution.py:23
  148.3 59.3 %all-gather.29.cloned.1.call-done = bf16[2,1,256,4096]{3,2,1,0:T(8,128)(2,1)} async-done(((bf16[2,1,256,128]{3,2,1,0:T(8,128)(2,1)}), bf16[2,1,256,4096]{3,2,1,0:T(8,128)(2,1)}) %all-gather.29.cloned.1.call-update) | async-done | bytes 4194320 | tf_op jit(solution)/shard_map/all_gather | solution.py:24
  207.6 2.7 fusion.12
  210.7 2.0 fusion.13
  212.7 33.2 %all-gather.23.cloned.1.call-done = bf16[2,1,4096,128]{3,2,1,0:T(8,128)(2,1)} async-done(((bf16[2,1,512,128]{3,2,1,0:T(8,128)(2,1)}), bf16[2,1,4096,128]{3,2,1,0:T(8,128)(2,1)}) %all-gather.23.cloned.1.call-update) | async-done | bytes 2097168 | tf_op jit(solution)/shard_map/all_gather | solution.py:23
  245.8 59.3 %all-gather.21.cloned.1.call-done = bf16[2,1,256,4096]{3,2,1,0:T(8,128)(2,1)} async-done(((bf16[2,1,256,128]{3,2,1,0:T(8,128)(2,1)}), bf16[2,1,256,4096]{3,2,1,0:T(8,128)(2,1)}) %all-gather.21.cloned.1.call-update) | async-done | bytes 4194320 | tf_op jit(solution)/shard_map/all_gather | solution.py:24
  305.1 2.7 fusion.4
  308.2 2.1 fusion.5
  310.4 33.2 %all-gather.19.cloned.1.call-done = bf16[2,1,4096,128]{3,2,1,0:T(8,128)(2,1)} async-done(((bf16[2,1,512,128]{3,2,1,0:T(8,128)(2,1)}), bf16[2,1,4096,128]{3,2,1,0:T(8,128)(2,1)}) %all-gather.19.cloned.1.call-update) | async-done | bytes 2097168 | tf_op jit(solution)/shard_map/all_gather | solution.py:23
  343.5 59.4 %all-gather.17.cloned.1.call-done = bf16[2,1,256,4096]{3,2,1,0:T(8,128)(2,1)} async-done(((bf16[2,1,256,128]{3,2,1,0:T(8,128)(2,1)}), bf16[2,1,256,4096]{3,2,1,0:T(8,128)(2,1)}) %all-gather.17.cloned.1.call-update) | async-done | bytes 4194320 | tf_op jit(solution)/shard_map/all_gather | solution.py:24
  403.0 2.7 fusion
  406.1 2.1 fusion.1
  408.6 0.7 fusion.23
  409.3 0.7 fusion.21
  410.2 1.5 copy-done.4
  411.7 0.7 fusion.19
  412.4 0.7 fusion.17
  413.2 1.5 copy-done.6
  414.7 0.7 fusion.27
  415.4 0.7 fusion.25
  416.1 0.9 copy-done.11
  417.0 0.7 fusion.31
  417.7 0.7 fusion.29
  418.5 1.0 pad_maximum_fusion
  (36 shorter events, 5.1 us)
Async XLA Ops:
  6.5 2.3 copy-start
  6.5 43.9 %all-gather.27.cloned.1.call-start = ((), (), s32[]{:S(2)}) async-start(), calls=%async_computation.5 | async-start | bytes 2359296 | tf_op jit(solution)/shard_map/all_gather | solution.py:23
  8.8 101.1 %all-gather.25.cloned.1.call-start = ((), (), s32[]{:S(2)}) async-start(), calls=%async_computation.4 | async-start | bytes 4325376 | tf_op jit(solution)/shard_map/all_gather | solution.py:24
  9.7 138.6 %all-gather.31.cloned.1.call-start = ((), (), s32[]{:S(2)}) async-start(), calls=%async_computation.7 | async-start | bytes 2359296 | tf_op jit(solution)/shard_map/all_gather | solution.py:23
  10.4 197.1 %all-gather.29.cloned.1.call-start = ((), (), s32[]{:S(2)}) async-start(), calls=%async_computation.6 | async-start | bytes 4325376 | tf_op jit(solution)/shard_map/all_gather | solution.py:24
  11.0 234.8 %all-gather.23.cloned.1.call-start = ((), (), s32[]{:S(2)}) async-start(), calls=%async_computation.3 | async-start | bytes 2359296 | tf_op jit(solution)/shard_map/all_gather | solution.py:23
  11.6 293.5 %all-gather.21.cloned.1.call-start = ((), (), s32[]{:S(2)}) async-start(), calls=%async_computation.2 | async-start | bytes 4325376 | tf_op jit(solution)/shard_map/all_gather | solution.py:24
  12.1 331.4 %all-gather.19.cloned.1.call-start = ((), (), s32[]{:S(2)}) async-start(), calls=%async_computation.1 | async-start | bytes 2359296 | tf_op jit(solution)/shard_map/all_gather | solution.py:23
  12.9 390.1 %all-gather.17.cloned.1.call-start = ((), (), s32[]{:S(2)}) async-start(), calls=%async_computation | async-start | bytes 4325376 | tf_op jit(solution)/shard_map/all_gather | solution.py:24
  109.8 3.1 copy-start.1
  207.6 3.1 copy-start.3
  305.1 3.1 copy-start.5
  308.2 99.9 %copy-start.8 = (bf16[2,1,4096,128]{3,2,1,0:T(8,128)(2,1)S(1)}, bf16[2,1,4096,128]{3,2,1,0:T(8,128)(2,1)}, u32[]{:S(2)}) copy-start(bf16[2,1,4096,128]{3,2,1,0:T(8,128)(2,1)} %all-gather.27.cloned.1.call-done) | copy-start | bytes 6291460
  403.0 3.1 copy-start.7
  406.1 2.5 copy-start.2
  408.6 1.6 copy-start.9
  409.3 2.3 copy-start.4
  411.7 1.6 copy-start.10
  412.4 2.3 copy-start.6
  415.4 1.6 copy-start.11
Sparse Core Ops, SparseCore 0:
  9.2 41.2 all-gather.26
  52.9 56.9 all-gather.24
  111.6 36.5 all-gather.30
  150.6 56.9 all-gather.28
  209.2 36.5 all-gather.22
  248.1 56.9 all-gather.20
  306.9 36.5 all-gather.18
  346.0 56.9 all-gather.16
where the time goes:
time: 427 us; the launch traced here: 426 us
  waiting for transfers between devices  378 us (89%)
  matrix products  24.5 us (6%)
  between operations  13.7 us (3%)
  local copies, waits for them, and re-layouts  9.26 us (2%)
    all_gather x4, waiting for transfers between devices, shards(): segment = lax.all_gather(panel, 'rec', axis=2, tiled=True)  237 us
    all_gather x4, waiting for transfers between devices, shards(): columns = lax.all_gather(block, 'shot', axis=1, tiled=True)  136 us
    dot_general x4, matrix products, complex_product(): jnp.dot(left_re, right_im, preferred_element_type=jnp.float32)  10.8 us
  transfers between devices with their start and end apart: 8, of which 8 were waited for; matrix products, arithmetic and copies ran while one was open for 4% of the time, Pallas kernels for 0%

commit v1 on v0

v1 whole, which is shorter than its diff:
```python
import jax
import jax.numpy as jnp
from jax import lax
from jax.experimental import pallas as pl
from jax.experimental.pallas import tpu as pltpu
from jax.sharding import PartitionSpec as P

MESH = pl.DeviceIdType.MESH
F = 4
NZ = 8
NQ = 16


def rec_of(x, y, c):
    return (y * 4 + x) * 2 + c


def kernel(p_ref, d_ref, o_ref, pall, dall, p_send, p_recv, sib_send, sib_recv, d_send, d_recv, local_sem):
    z = lax.axis_index("shot")
    r = lax.axis_index("rec")
    c = lax.rem(r, 2)
    x = lax.rem(r // 2, 4)
    y = r // 8
    s = lax.rem(x + y, 4)
    last, first = s // 3, (3 - s) // 3
    sibling = (z, rec_of(x, y, 1 - c))
    up, down = (lax.rem(z + 1, NZ), r), (lax.rem(z + NZ - 1, NZ), r)

    def at(dx, dy):
        return (z, rec_of(lax.rem(x + dx + 4, 4), lax.rem(y + dy + 4, 4), c))

    targets = (at(1 - last, last), at(first - 1, -first), at(last, 1 - last), at(-first, first - 1))
    place = (y * 4 + s, x * 4 + s)

    def owner(ring, k):
        i = lax.rem(place[ring // 2] + (NQ - k if ring % 2 == 0 else k), NQ)
        major = i // 4
        minor = lax.rem(lax.rem(i, 4) - major + 4, 4)
        return rec_of(minor, major, c) if ring < 2 else rec_of(major, minor, c)

    barrier = pltpu.get_barrier_semaphore()
    for other in (up, down, sibling) + targets:
        pl.semaphore_signal(barrier, inc=1, device_id=other, device_id_type=MESH)
    pl.semaphore_wait(barrier, 7)

    def d_copy(direction, source, slot, chunk):
        f = chunk // 2 if direction == 0 else 3 - chunk // 2
        part = lax.rem(chunk, 2)
        src = d_ref.at[part, f] if source is None else dall.at[source, part, f]
        return pltpu.make_async_remote_copy(
            src_ref=src,
            dst_ref=dall.at[slot, part, f],
            send_sem=d_send.at[direction],
            recv_sem=d_recv.at[direction, slot, chunk],
            device_id=(up, down)[direction],
            device_id_type=MESH,
        )

    def slot_of(direction, step):
        return step if direction == 0 else (step + 4 if not isinstance(step, int) or step < 4 else 4)

    own_d = pltpu.make_async_copy(d_ref, dall.at[0], local_sem.at[0])
    own_d.start()

    @pl.loop(0, 8)
    def _(chunk):
        for direction in (0, 1):
            d_copy(direction, None, slot_of(direction, 1), chunk).start()

    def p_copy(ring, part, k):
        slot = owner(ring, k)
        return pltpu.make_async_remote_copy(
            src_ref=pall.at[ring, part, slot],
            dst_ref=pall.at[ring, part, slot],
            send_sem=p_send.at[ring, part],
            recv_sem=p_recv.at[ring, part, k],
            device_id=targets[ring],
            device_id_type=MESH,
        )

    def sib_copy(ring, part, k):
        slot = owner(ring, k)
        return pltpu.make_async_remote_copy(
            src_ref=pall.at[ring, part, slot],
            dst_ref=pall.at[ring, part, slot],
            send_sem=sib_send,
            recv_sem=sib_recv,
            device_id=sibling,
            device_id_type=MESH,
        )

    own_p = [
        pltpu.make_async_copy(p_ref.at[part, f], pall.at[f, part, r], local_sem.at[1 + 2 * f + part])
        for f in range(F)
        for part in (0, 1)
    ]
    for copy in own_p:
        copy.start()
    for copy in own_p:
        copy.wait()

    def p_step(k):
        for part in (0, 1):
            for ring in range(F):
                p_copy(ring, part, k).start()
                sib_copy(ring, part, k).start()

    def p_wait(k):
        for part in (0, 1):
            for ring in range(F):
                p_copy(ring, part, k).wait_recv()

    def d_pass(t):
        step, chunk = 1 + t // 8, lax.rem(t, 8)
        for direction in (0, 1):
            slot = slot_of(direction, step)
            d_copy(direction, None, slot, chunk).wait_recv()
            d_copy(direction, slot, slot + 1, chunk).start()

    p_step(0)

    @pl.loop(1, NQ - 1)
    def _(k):
        for part in (0, 1):
            for ring in range(F):
                p_copy(ring, part, k - 1).wait_recv()
                p_copy(ring, part, k).start()
                sib_copy(ring, part, k).start()
        d_pass(k - 1)

    p_wait(NQ - 2)
    for part in (0, 1):
        for ring in range(F):
            sib_copy(ring, part, NQ - 1).start()
    d_pass(14)
    d_pass(15)
    own_d.wait()

    def add(slot, f, where, start=False):
        base = where * 4
        left = [
            jnp.concatenate([pall[f, part, base + i] for i in range(4)], axis=1) for part in (0, 1)
        ]
        re, im = dall[slot, 0, f], dall[slot, 1, f]
        a = jnp.dot(left[0], jnp.concatenate([re, im], axis=1), preferred_element_type=jnp.float32)
        b = jnp.dot(left[1], jnp.concatenate([im, re], axis=1), preferred_element_type=jnp.float32)
        real = a[:, :128] - b[:, :128]
        imag = a[:, 128:] + b[:, 128:]
        if start:
            o_ref[0, f] = real
            o_ref[1, f] = imag
        else:
            o_ref[0, f] += real
            o_ref[1, f] += imag

    half = pall.at[:, :, pl.ds(0, NQ)]
    whole = pltpu.make_async_remote_copy(
        src_ref=half, dst_ref=half, send_sem=sib_send, recv_sem=sib_recv, device_id=sibling, device_id_type=MESH
    )
    whole.wait_recv()

    @pl.loop(0, F)
    def _(f):
        add(0, f, z, start=True)

    def add_block(slot, where):
        @pl.loop(0, F)
        def _(f):
            add(slot, f, where)

    for step in (1, 2):
        add_block(step, lax.rem(z + NZ - step, NZ))
        add_block(step + 4, lax.rem(z + step, NZ))

    for direction in (0, 1):
        for chunk in range(8):
            pass

    def tail(chunk_pair, forward):
        for direction in (0, 1):
            slot = 3 if direction == 0 else 7
            for part in (0, 1):
                chunk = chunk_pair * 2 + part
                d_copy(direction, None, slot, chunk).wait_recv()
                if forward:
                    d_copy(direction, slot, 4, chunk).start()
        for direction in (0, 1):
            f = chunk_pair if direction == 0 else 3 - chunk_pair
            if direction == 0:
                add(3, f, lax.rem(z + NZ - 3, NZ))
            else:
                add(7, f, lax.rem(z + 3, NZ))

    @pl.loop(0, 2)
    def _(i):
        tail(i, True)

    @pl.loop(2, 4)
    def _(i):
        tail(i, False)

    @pl.loop(0, 2)
    def _(i):
        for direction in (0, 1):
            for part in (0, 1):
                d_copy(direction, None, 4, i * 2 + part).wait_recv()
            add(4, i if direction == 0 else 3 - i, lax.rem(z + 4, NZ))

    whole.wait_send()
    for ring in range(F):
        for part in (0, 1):
            ref = pall.at[ring, part, pl.ds(0, NQ - 1)]
            pltpu.make_async_remote_copy(
                src_ref=ref,
                dst_ref=ref,
                send_sem=p_send.at[ring, part],
                recv_sem=p_recv.at[ring, part, 0],
                device_id=targets[ring],
                device_id_type=MESH,
            ).wait_send()
    for direction in (0, 1):
        for ref in (dall.at[pl.ds(0, 3)], dall.at[0, :, pl.ds(0, 2)]):
            pltpu.make_async_remote_copy(
                src_ref=ref,
                dst_ref=ref,
                send_sem=d_send.at[direction],
                recv_sem=d_recv.at[direction, 1, 0],
                device_id=(up, down)[direction],
                device_id_type=MESH,
            ).wait_send()


def shards(primaries, recorded):
    return pl.pallas_call(
        kernel,
        out_shape=jax.ShapeDtypeStruct((2, F, 256, 128), jnp.float32),
        in_specs=[pl.BlockSpec(memory_space=pl.ANY)] * 2,
        out_specs=pl.BlockSpec(memory_space=pltpu.VMEM),
        scratch_shapes=[
            pltpu.VMEM((F, 2, 2 * NQ, 256, 128), jnp.bfloat16),
            pltpu.VMEM((NZ, 2, F, 512, 128), jnp.bfloat16),
            pltpu.SemaphoreType.DMA((F, 2)),
            pltpu.SemaphoreType.DMA((F, 2, NQ - 1)),
            pltpu.SemaphoreType.DMA,
            pltpu.SemaphoreType.DMA,
            pltpu.SemaphoreType.DMA((2,)),
            pltpu.SemaphoreType.DMA((2, NZ, 8)),
            pltpu.SemaphoreType.DMA((9,)),
        ],
        compiler_params=pltpu.CompilerParams(
            collective_id=0, has_side_effects=True, vmem_limit_bytes=56 * 1024 * 1024
        ),
        cost_estimate=pl.CostEstimate(flops=4294967296, bytes_accessed=3 << 20, transcendentals=0),
    )(primaries, recorded)


def solution(mesh):
    placed = (P(None, None, "shot", "rec"), P(None, None, "shot", "rec"))
    return jax.shard_map(
        shards, mesh=mesh, in_specs=placed, out_specs=P(None, None, "shot", "rec"), check_vma=False
    )
```

time: 427 us -> 98 us (0.23)
  waiting for transfers between devices: 378 us -> 0 us
  Pallas kernels: 0 us -> 95.6 us
  matrix products: 24.5 us -> 0 us
  between operations: 13.7 us -> 0.01 us
  local copies, waits for them, and re-layouts: 9.26 us -> 2.27 us
    all_gather x8 -> x0, waiting for transfers between devices: 374 us -> none  [the longest x4 237 us: shards(): segment = lax.all_gather(panel, 'rec', axis=2, tiled=True)]
    pallas_call x0 -> x1, Pallas kernels: none -> 95.6 us  [shards(): pl.pallas_call(kernel, out_shape=jax.ShapeDtypeStruct((2, F, 256, 128), j...]
    dot_general x16 -> x0, matrix products: 24.5 us -> none  [the longest x4 10.8 us: complex_product(): jnp.dot(left_re, right_im, preferred_element_type=jnp.float32)]
  transfers between devices with their start and end apart: 8 -> 0, of which waited for: 8 -> 0; matrix products, arithmetic and copies ran while one was open for 4% -> 0% of each run, Pallas kernels for 0% -> 0%
where the time goes in v1:
time: 98 us; the launch traced here: 97.9 us
  Pallas kernels  95.6 us (98%)
  local copies, waits for them, and re-layouts  2.27 us (2%)
    pallas_call x1, Pallas kernels, shards(): pl.pallas_call(kernel, out_shape=jax.ShapeDtypeStruct((2, F, 256, 128), j...  95.6 us
    unnamed x1, local copies, waits for them, and re-layouts  2.27 us

profile of v1, /device:TPU:1, one launch (start us, length us, event | category | flops | bytes accessed | tf_op | source)
XLA Modules:
  0.0 97.9 jit_solution(16371157077949078167)
XLA Ops:
  0.0 95.6 %shard_map.28 = f32[2,4,256,128]{3,2,1,0:T(8,128)} custom-call(bf16[2,4,256,128]{3,2,1,0:T(8,128)(2,1)} %p_ref.1, bf16[2,4,512,128]{3,2,1,0:T(8,128)(2,1)} %d_ref.1), custom_call_target="tpu_custom_call" | custom-call | flops 4294967296 | bytes 3145728 | tf_op jit(solution)/shard_map/pallas_call | solution.py:234
  95.6 2.3 %copy.4 = f32[2,4,256,128]{3,2,1,0:T(8,128)} copy(f32[2,4,256,128]{3,2,1,0:T(8,128)} %shard_map.28) | data formatting | bytes 2097152

commit v2 on v0

v2 whole, which is shorter than its diff:
```python
import jax
import jax.numpy as jnp
from jax import lax
from jax.experimental import pallas as pl
from jax.experimental.pallas import tpu as pltpu
from jax.sharding import PartitionSpec as P

MESH = pl.DeviceIdType.MESH
F = 4
NZ = 8
NQ = 16
OWN12, HELP1, HELP2, OWN03 = 0, 1, 2, 3


def rec_of(x, y, c):
    return (y * 4 + x) * 2 + c


def kernel(
    p_ref, d_ref, o_ref, pall, dall, cpart, crecv,
    stage, help_send, help_recv, stage_send, stage_recv, own_send, own_recv, p_send, p_recv, sib_send, sib_recv, d_send, d_recv, c_send, c_recv, local_sem,
):
    z = lax.axis_index("shot")
    r = lax.axis_index("rec")
    c = lax.rem(r, 2)
    x = lax.rem(r // 2, 4)
    y = r // 8

    def plane(dz):
        return lax.rem(z + (dz + NZ), NZ)

    def rec(dx, dy):
        return rec_of(lax.rem(x + dx + 4, 4), lax.rem(y + dy + 4, 4), c)

    def freq(role):
        return lax.rem(z + (4 - role), 4)

    sibling = (z, rec_of(x, y, 1 - c))
    up, down, up2, down2 = ((plane(d), r) for d in (1, -1, 2, -2))
    across = (z, rec(0, 2))
    sides = ((z, rec(1, 0)), (z, rec(-1, 0))), ((z, rec(0, 1)), (z, rec(0, -1)))

    barrier = pltpu.get_barrier_semaphore()
    partners = (sibling, up, down, up2, down2, across) + sides[0] + sides[1]
    for other in partners:
        pl.semaphore_signal(barrier, inc=1, device_id=other, device_id_type=MESH)
    pl.semaphore_wait(barrier, len(partners))

    def remote(src, dst, send, recv, device):
        return pltpu.make_async_remote_copy(
            src_ref=src, dst_ref=dst, send_sem=send, recv_sem=recv, device_id=device, device_id_type=MESH
        )

    delta = lax.rem(r // 4 + NZ - z, NZ)
    delta_across = lax.rem(delta + 4, NZ)

    def is_in(values, where):
        hit = jnp.int32(0)
        for v in values:
            hit = hit + jnp.where(where == v, 1, 0)
        return hit

    AWAY = ((4, 5, 6, 7), (3, 4, 5, 6), (2, 3, 4, 5), (1, 2, 3, 4))
    HELPER = (down, down2, up2, up)
    HELP = (HELP1, HELP2, HELP2, HELP1)
    TURN = (7, 6, -1, -1)

    def moves(role, part, where):
        away = is_in(AWAY[role], where)
        turn = is_in((TURN[role],), where)
        turned = turn if part == 0 else 1 - turn
        return away * turned, away * (1 - turned)

    def help_copy(role, part, staged):
        src = stage.at[role, part] if staged else p_ref.at[part, freq(role)]
        n = 1 if staged else 0
        group = HELP[role]
        return remote(
            src, pall.at[group, part, r], help_send.at[n, role, part], help_recv.at[group, part], HELPER[role]
        )

    def stage_copy(role, part):
        return remote(
            p_ref.at[part, freq(role)], stage.at[role, part], stage_send.at[role, part], stage_recv.at[role, part], across
        )

    def own_copy(role):
        if role == 0:
            mine, dy = is_in((0, 1, 2, 3), delta), 0
        elif role == 3:
            mine, dy = is_in((0, 5, 6, 7), delta), is_in((0,), delta) * 2
        elif role == 1:
            mine, dy = is_in((7, 0, 1, 2), delta), 0
        else:
            mine = is_in((6, 7, 0, 1), delta)
            dy = is_in((7,), delta) * 3 + is_in((0,), delta) * 2 + is_in((1,), delta)
        group = OWN03 if role in (0, 3) else OWN12
        target = rec_of(x, lax.rem(y + dy, 4), c)
        src, dst = p_ref.at[:, freq(role)], pall.at[group, :, target]
        stays = mine * jnp.where(dy == 0, 1, 0)
        leaves = mine * jnp.where(dy == 0, 0, 1)

        def local():
            return pltpu.make_async_copy(src, dst, own_recv.at[group])

        def away():
            return remote(src, dst, own_send.at[role], own_recv.at[group], (z, target))

        return stays, leaves, local, away

    def when(condition, action):
        @pl.when(condition == 1)
        def _():
            action()

    def place_direct():
        for role in (3, 0, 2, 1):
            for part in (0, 1):
                when(moves(role, part, delta)[1], lambda: help_copy(role, part, False).start())

    def place_across():
        for role in (3, 0, 2, 1):
            for part in (1, 0):
                when(moves(role, part, delta)[0], lambda: stage_copy(role, part).start())

    def place_own(roles):
        for role in roles:
            stays, leaves, local, away = own_copy(role)
            when(stays, lambda: local().start())
            when(leaves, lambda: away().start())

    def place_staged():
        for role in (3, 0, 2, 1):
            for part in (1, 0):

                def pass_on():
                    stage_copy(role, part).wait_recv()
                    help_copy(role, part, True).start()

                when(moves(role, part, delta_across)[0], pass_on)

    def place_sent():
        for role in range(4):
            for part in (0, 1):
                when(moves(role, part, delta)[1], lambda: help_copy(role, part, False).wait_send())
                when(moves(role, part, delta)[0], lambda: stage_copy(role, part).wait_send())
                when(moves(role, part, delta_across)[0], lambda: help_copy(role, part, True).wait_send())
            leaves, away = own_copy(role)[1], own_copy(role)[3]
            when(leaves, lambda: away().wait_send())

    def piece_wait(group, part):
        if group in (HELP1, HELP2):
            ref = pall.at[group, part, r]
            remote(ref, ref, help_send.at[0, 0, part], help_recv.at[group, part], sibling).wait_recv()
        elif part == 0:
            ref = pall.at[group, :, r]
            pltpu.make_async_copy(ref, ref, own_recv.at[group]).wait()

    def d_copy(role, pos, part, upwards):
        f = freq(role)
        src = d_ref.at[part, f] if pos == role else dall.at[f, pos, part]
        way = 0 if upwards else 1
        return remote(src, dall.at[f, pos, part], d_send.at[way], d_recv.at[f, pos, part], up if upwards else down)

    def d_wait(role, pos):
        f = freq(role)
        for part in (0, 1):
            ref = dall.at[f, pos, part]
            remote(ref, ref, d_send.at[0], d_recv.at[f, pos, part], up).wait_recv()

    def d_forward(role, pos, upwards):
        d_wait(role, pos)
        for part in (0, 1):
            d_copy(role, pos, part, upwards).start()

    def d_own(i):
        for part in (0, 1):
            d_copy(i, i, part, True).start()
            d_copy(3 - i, 3 - i, part, False).start()

    own_d = [
        pltpu.make_async_copy(d_ref.at[:, freq(role)], dall.at[freq(role), role], local_sem.at[role]) for role in range(4)
    ]

    def slot(part, a, b):
        return rec(a, b) if part == 0 else rec(b, a)

    def p_copy(group, part, a, b, index, device, half=None):
        ref = pall.at[group, part, slot(part, a, b)]
        if half is not None:
            ref = ref.at[pl.ds(half * 128, 128)]
        return remote(ref, ref, p_send.at[group, part], p_recv.at[group, part, index], device)

    def share(group, part, a, b):
        ref = pall.at[group, part, slot(part, a, b)]
        remote(ref, ref, sib_send.at[group], sib_recv.at[group], sibling).start()

    def first(part):
        return sides[part]

    def second(part):
        return sides[1 - part]

    LINE = (0, -1, 1, 2)

    def stage1(group, parts=(0, 1)):
        for part in parts:
            piece_wait(group, part)
            for way in (0, 1):
                p_copy(group, part, 0, 0, way, first(part)[way]).start()
            for way in (0, 1):
                p_copy(group, part, 0, 0, 4 + way, second(part)[way]).start()
            share(group, part, 0, 0)

    def stage2(group):
        for way in (0, 1):
            a = LINE[1 + way]
            for part in (0, 1):
                p_copy(group, part, a, 0, way, sibling).wait_recv()
                p_copy(group, part, a, 0, 2 + way, first(part)[way], half=way).start()
                for turn in (0, 1):
                    p_copy(group, part, a, 0, 4 + 4 * (1 + way) + turn, second(part)[turn]).start()
                share(group, part, a, 0)

    def stage2b(group):
        for part in (0, 1):
            for way in (0, 1):
                p_copy(group, part, 2, 0, 2 + way, sibling, half=way).wait_recv()
            for turn in (0, 1):
                p_copy(group, part, 2, 0, 16 + turn, second(part)[turn]).start()
            share(group, part, 2, 0)

    def stage3(group):
        for i in range(4):
            for way in (0, 1):
                b = LINE[1 + way]
                for part in (0, 1):
                    p_copy(group, part, LINE[i], b, 4 + 4 * i + way, sibling).wait_recv()
                    p_copy(group, part, LINE[i], b, 6 + 4 * i + way, second(part)[way], half=way).start()
                    share(group, part, LINE[i], b)

    def stage4(group):
        for i in range(4):
            for part in (0, 1):
                for way in (0, 1):
                    p_copy(group, part, LINE[i], 2, 6 + 4 * i + way, sibling, half=way).wait_recv()
                share(group, part, LINE[i], 2)

    def shared(group):
        ref = pall.at[group, :, pl.ds(0, NQ)]
        return remote(ref, ref, sib_send.at[group], sib_recv.at[group], sibling)

    def home(group, part, role, pos):
        if group in (OWN12, OWN03):
            return plane(((0, 1, 2, 3), (-1, 0, 1, 2), (-2, -3, 4, 3), (-3, -2, -1, 4))[role][pos])
        if role == 0:
            return plane(pos if part == 0 else pos + 4)
        return plane((-3, -2, -1, 4)[pos] if part == 0 else (1, 2, 3, 0)[pos])

    def product(group, role, pos):
        f = freq(role)
        left = []
        for part in (0, 1):
            base = home(group, part, role, pos) * 4
            left.append(jnp.concatenate([pall[group, part, base + i] for i in range(4)], axis=1))
        re, im = dall[f, pos, 0], dall[f, pos, 1]
        u = jnp.dot(left[0], jnp.concatenate([re, im], axis=1), preferred_element_type=jnp.float32)
        v = jnp.dot(left[1], jnp.concatenate([im, re], axis=1), preferred_element_type=jnp.float32)
        return u[:, :128] - v[:, :128], u[:, 128:] + v[:, 128:]

    def help_with(group, role, n):
        index = (0 if role == 0 else 1) + (0 if group == HELP1 else 2)
        for part, value in enumerate(product(group, role, n if role == 0 else 3 - n)):
            if n == 0:
                cpart[index, part] = value
            else:
                cpart[index, part] += value
        if n < 3:
            return
        f = freq(role)
        near, far = (down, down2) if role == 0 else (up, up2)
        for part in (0, 1):
            remote(
                cpart.at[index, part], crecv.at[f, part], c_send.at[index], c_recv.at[f, part],
                near if group == HELP1 else far,
            ).start()

    def own_products(group, role, positions, start):
        f = freq(role)
        for n, pos in enumerate(positions):
            for part, value in enumerate(product(group, role, pos)):
                if start and n == 0:
                    o_ref[part, f] = value
                else:
                    o_ref[part, f] += value

    place_own((0, 3))
    place_direct()
    place_across()
    place_own((1, 2))
    d_own(0)
    for copy in own_d:
        copy.start()
    stage1(OWN03)
    place_staged()
    d_own(1)
    d_own(2)
    stage1(HELP1, (0,))
    stage2(OWN03)
    stage1(HELP2, (0,))
    stage1(HELP1, (1,))
    stage2(HELP1)
    stage2b(OWN03)
    stage1(HELP2, (1,))
    stage2b(HELP1)
    stage3(OWN03)
    stage2(HELP2)
    d_forward(1, 0, True)
    d_forward(2, 3, False)
    stage3(HELP1)
    stage2b(HELP2)
    d_forward(2, 1, True)
    d_forward(1, 2, False)
    stage1(OWN12)
    stage4(OWN03)
    stage3(HELP2)
    stage2(OWN12)
    stage4(HELP1)
    d_forward(2, 0, True)
    d_forward(1, 3, False)
    stage2b(OWN12)
    stage4(HELP2)
    stage3(OWN12)
    for copy in own_d:
        copy.wait()
    shared(HELP2).wait_recv()
    shared(HELP1).wait_recv()
    for n in range(4):
        if n > 0:
            d_wait(0, n)
            d_wait(3, 3 - n)
        for group in (HELP2, HELP1):
            for role in (0, 3):
                help_with(group, role, n)
    stage4(OWN12)
    shared(OWN03).wait_recv()
    own_products(OWN03, 0, (0, 1, 2, 3), True)
    own_products(OWN03, 3, (0, 1, 2, 3), True)
    shared(OWN12).wait_recv()
    own_products(OWN12, 1, (0, 1, 2, 3), True)
    own_products(OWN12, 2, (0, 1, 2, 3), True)
    for role in (0, 3, 1, 2):
        f = freq(role)
        for part in (0, 1):
            ref = crecv.at[f, part]
            remote(ref, ref, c_send.at[0], c_recv.at[f, part], up).wait_recv()
            o_ref[part, f] += crecv[f, part]

    for index in range(4):
        remote(cpart.at[index], cpart.at[index], c_send.at[index], c_recv.at[0, 0], up).wait_send()
    for group in range(4):
        shared(group).wait_send()
        for part in (0, 1):
            ref = pall.at[group, part, pl.ds(0, NQ - 1)]
            remote(ref, ref, p_send.at[group, part], p_recv.at[group, part, 0], sibling).wait_send()
    for way in (0, 1):
        ref = dall.at[pl.ds(0, 3), pl.ds(0, 2)]
        remote(ref, ref, d_send.at[way], d_recv.at[0, 0, 0], up).wait_send()
    place_sent()


def shards(primaries, recorded):
    return pl.pallas_call(
        kernel,
        out_shape=jax.ShapeDtypeStruct((2, F, 256, 128), jnp.float32),
        in_specs=[pl.BlockSpec(memory_space=pl.ANY)] * 2,
        out_specs=pl.BlockSpec(memory_space=pltpu.VMEM),
        scratch_shapes=[
            pltpu.VMEM((4, 2, 2 * NQ, 256, 128), jnp.bfloat16),
            pltpu.VMEM((F, 4, 2, 512, 128), jnp.bfloat16),
            pltpu.VMEM((4, 2, 256, 128), jnp.float32),
            pltpu.VMEM((F, 2, 256, 128), jnp.float32),
            pltpu.VMEM((4, 2, 256, 128), jnp.bfloat16),
            pltpu.SemaphoreType.DMA((2, 4, 2)),
            pltpu.SemaphoreType.DMA((4, 2)),
            pltpu.SemaphoreType.DMA((4, 2)),
            pltpu.SemaphoreType.DMA((4, 2)),
            pltpu.SemaphoreType.DMA((4,)),
            pltpu.SemaphoreType.DMA((4,)),
            pltpu.SemaphoreType.DMA((4, 2)),
            pltpu.SemaphoreType.DMA((4, 2, 20)),
            pltpu.SemaphoreType.DMA((4,)),
            pltpu.SemaphoreType.DMA((4,)),
            pltpu.SemaphoreType.DMA((2,)),
            pltpu.SemaphoreType.DMA((F, 4, 2)),
            pltpu.SemaphoreType.DMA((4,)),
            pltpu.SemaphoreType.DMA((F, 2)),
            pltpu.SemaphoreType.DMA((4,)),
        ],
        compiler_params=pltpu.CompilerParams(
            collective_id=0, has_side_effects=True, vmem_limit_bytes=56 * 1024 * 1024
        ),
        cost_estimate=pl.CostEstimate(flops=4294967296, bytes_accessed=3 << 20, transcendentals=0),
    )(primaries, recorded)


def solution(mesh):
    placed = (P(None, None, "shot", "rec"), P(None, None, "shot", "rec"))
    return jax.shard_map(
        shards, mesh=mesh, in_specs=placed, out_specs=P(None, None, "shot", "rec"), check_vma=False
    )
```

time: 427 us -> 86.9 us (0.20)
  waiting for transfers between devices: 378 us -> 0 us
  Pallas kernels: 0 us -> 84.5 us
  matrix products: 24.5 us -> 0 us
  between operations: 13.7 us -> 0.01 us
  local copies, waits for them, and re-layouts: 9.26 us -> 2.27 us
    all_gather x8 -> x0, waiting for transfers between devices: 374 us -> none  [the longest x4 237 us: shards(): segment = lax.all_gather(panel, 'rec', axis=2, tiled=True)]
    pallas_call x0 -> x1, Pallas kernels: none -> 84.5 us  [shards(): pl.pallas_call(kernel, out_shape=jax.ShapeDtypeStruct((2, F, 256, 128), j...]
    dot_general x16 -> x0, matrix products: 24.5 us -> none  [the longest x4 10.8 us: complex_product(): jnp.dot(left_re, right_im, preferred_element_type=jnp.float32)]
  transfers between devices with their start and end apart: 8 -> 0, of which waited for: 8 -> 0; matrix products, arithmetic and copies ran while one was open for 4% -> 0% of each run, Pallas kernels for 0% -> 0%
where the time goes in v2:
time: 86.9 us; the launch traced here: 86.7 us
  Pallas kernels  84.5 us (97%)
  local copies, waits for them, and re-layouts  2.27 us (3%)
    pallas_call x1, Pallas kernels, shards(): pl.pallas_call(kernel, out_shape=jax.ShapeDtypeStruct((2, F, 256, 128), j...  84.5 us
    unnamed x1, local copies, waits for them, and re-layouts  2.27 us

profile of v2, /device:TPU:1, one launch (start us, length us, event | category | flops | bytes accessed | tf_op | source)
XLA Modules:
  0.0 86.7 jit_solution(6714863756711516435)
XLA Ops:
  0.0 84.5 %shard_map.28 = f32[2,4,256,128]{3,2,1,0:T(8,128)} custom-call(bf16[2,4,256,128]{3,2,1,0:T(8,128)(2,1)} %p_ref.1, bf16[2,4,512,128]{3,2,1,0:T(8,128)(2,1)} %d_ref.1), custom_call_target="tpu_custom_call" | custom-call | flops 4294967296 | bytes 3145728 | tf_op jit(solution)/shard_map/pallas_call | solution.py:373
  84.5 2.3 %copy.4 = f32[2,4,256,128]{3,2,1,0:T(8,128)} copy(f32[2,4,256,128]{3,2,1,0:T(8,128)} %shard_map.28) | data formatting | bytes 2097152

commit v3 on v2

--- a/solution.py
+++ b/solution.py
@@ -148,11 +148,14 @@
             leaves, away = own_copy(role)[1], own_copy(role)[3]
             when(leaves, lambda: away().wait_send())
 
+    seen = []
+
     def piece_wait(group, part):
         if group in (HELP1, HELP2):
             ref = pall.at[group, part, r]
             remote(ref, ref, help_send.at[0, 0, part], help_recv.at[group, part], sibling).wait_recv()
-        elif part == 0:
+        elif group not in seen:
+            seen.append(group)
             ref = pall.at[group, :, r]
             pltpu.make_async_copy(ref, ref, own_recv.at[group]).wait()
 
@@ -212,36 +215,36 @@
                 p_copy(group, part, 0, 0, 4 + way, second(part)[way]).start()
             share(group, part, 0, 0)
 
-    def stage2(group):
+    def stage2(group, parts=(0, 1)):
         for way in (0, 1):
             a = LINE[1 + way]
-            for part in (0, 1):
+            for part in parts:
                 p_copy(group, part, a, 0, way, sibling).wait_recv()
                 p_copy(group, part, a, 0, 2 + way, first(part)[way], half=way).start()
                 for turn in (0, 1):
                     p_copy(group, part, a, 0, 4 + 4 * (1 + way) + turn, second(part)[turn]).start()
                 share(group, part, a, 0)
 
-    def stage2b(group):
-        for part in (0, 1):
+    def stage2b(group, parts=(0, 1)):
+        for part in parts:
             for way in (0, 1):
                 p_copy(group, part, 2, 0, 2 + way, sibling, half=way).wait_recv()
             for turn in (0, 1):
                 p_copy(group, part, 2, 0, 16 + turn, second(part)[turn]).start()
             share(group, part, 2, 0)
 
-    def stage3(group):
+    def stage3(group, parts=(0, 1)):
         for i in range(4):
             for way in (0, 1):
                 b = LINE[1 + way]
-                for part in (0, 1):
+                for part in parts:
                     p_copy(group, part, LINE[i], b, 4 + 4 * i + way, sibling).wait_recv()
                     p_copy(group, part, LINE[i], b, 6 + 4 * i + way, second(part)[way], half=way).start()
                     share(group, part, LINE[i], b)
 
-    def stage4(group):
+    def stage4(group, parts=(0, 1)):
         for i in range(4):
-            for part in (0, 1):
+            for part in parts:
                 for way in (0, 1):
                     p_copy(group, part, LINE[i], 2, 6 + 4 * i + way, sibling, half=way).wait_recv()
                 share(group, part, LINE[i], 2)
@@ -268,87 +271,113 @@
         v = jnp.dot(left[1], jnp.concatenate([im, re], axis=1), preferred_element_type=jnp.float32)
         return u[:, :128] - v[:, :128], u[:, 128:] + v[:, 128:]
 
-    def help_with(group, role, n):
+    def help_step(group, role, n):
         index = (0 if role == 0 else 1) + (0 if group == HELP1 else 2)
         for part, value in enumerate(product(group, role, n if role == 0 else 3 - n)):
             if n == 0:
                 cpart[index, part] = value
             else:
                 cpart[index, part] += value
-        if n < 3:
-            return
-        f = freq(role)
-        near, far = (down, down2) if role == 0 else (up, up2)
-        for part in (0, 1):
-            remote(
-                cpart.at[index, part], crecv.at[f, part], c_send.at[index], c_recv.at[f, part],
-                near if group == HELP1 else far,
-            ).start()
-
-    def own_products(group, role, positions, start):
-        f = freq(role)
-        for n, pos in enumerate(positions):
-            for part, value in enumerate(product(group, role, pos)):
-                if start and n == 0:
-                    o_ref[part, f] = value
-                else:
-                    o_ref[part, f] += value
-
+
+    def help_first():
+        for copy in own_d:
+            copy.wait()
+        shared(HELP1).wait_recv()
+        shared(HELP2).wait_recv()
+        for n in range(3):
+            if n > 0:
+                d_wait(0, n)
+                d_wait(3, 3 - n)
+            for group in (HELP2, HELP1):
+                for role in (0, 3):
+                    help_step(group, role, n)
+
+    def help_last(group):
+        for role in (0, 3):
+            if group == HELP2:
+                d_wait(role, 3 - role)
+            help_step(group, role, 3)
+            index = (0 if role == 0 else 1) + (0 if group == HELP1 else 2)
+            f = freq(role)
+            near, far = (down, down2) if role == 0 else (up, up2)
+            for part in (0, 1):
+                remote(
+                    cpart.at[index, part], crecv.at[f, part], c_send.at[index], c_recv.at[f, part],
+                    near if group == HELP1 else far,
+                ).start()
+
+    def own_block(group):
+        shared(group).wait_recv()
+        for role in (0, 3) if group == OWN03 else (1, 2):
+            f = freq(role)
+            for pos in range(4):
+                for part, value in enumerate(product(group, role, pos)):
+                    if pos == 0:
+                        o_ref[part, f] = value
+                    else:
+                        o_ref[part, f] += value
+
+    place_across()
+    place_direct()
     place_own((0, 3))
-    place_direct()
-    place_across()
     place_own((1, 2))
-    d_own(0)
     for copy in own_d:
         copy.start()
-    stage1(OWN03)
+    d_own(0)
+    stage1(HELP1, (0,))
     place_staged()
+    stage1(HELP2, (0,))
+    stage1(OWN03, (0,))
     d_own(1)
+    stage2(HELP1, (0,))
+    stage1(HELP1, (1,))
     d_own(2)
-    stage1(HELP1, (0,))
-    stage2(OWN03)
-    stage1(HELP2, (0,))
-    stage1(HELP1, (1,))
-    stage2(HELP1)
-    stage2b(OWN03)
     stage1(HELP2, (1,))
-    stage2b(HELP1)
-    stage3(OWN03)
-    stage2(HELP2)
+    stage2(HELP2, (0,))
+    stage2(HELP1, (1,))
+    stage2b(HELP1, (0,))
+    stage2(HELP2, (1,))
     d_forward(1, 0, True)
     d_forward(2, 3, False)
-    stage3(HELP1)
-    stage2b(HELP2)
+    stage2b(HELP2, (0,))
+    stage2b(HELP1, (1,))
     d_forward(2, 1, True)
     d_forward(1, 2, False)
-    stage1(OWN12)
-    stage4(OWN03)
-    stage3(HELP2)
-    stage2(OWN12)
-    stage4(HELP1)
+    stage3(HELP1, (0,))
+    stage2b(HELP2, (1,))
+    stage3(HELP2, (0,))
+    stage3(HELP1, (1,))
+    stage3(HELP2, (1,))
+    stage1(OWN12, (0,))
     d_forward(2, 0, True)
     d_forward(1, 3, False)
-    stage2b(OWN12)
-    stage4(HELP2)
-    stage3(OWN12)
-    for copy in own_d:
-        copy.wait()
-    shared(HELP2).wait_recv()
-    shared(HELP1).wait_recv()
-    for n in range(4):
-        if n > 0:
-            d_wait(0, n)
-            d_wait(3, 3 - n)
-        for group in (HELP2, HELP1):
-            for role in (0, 3):
-                help_with(group, role, n)
-    stage4(OWN12)
-    shared(OWN03).wait_recv()
-    own_products(OWN03, 0, (0, 1, 2, 3), True)
-    own_products(OWN03, 3, (0, 1, 2, 3), True)
-    shared(OWN12).wait_recv()
-    own_products(OWN12, 1, (0, 1, 2, 3), True)
-    own_products(OWN12, 2, (0, 1, 2, 3), True)
+    stage1(OWN03, (1,))
+    stage4(HELP2, (0,))
+    stage4(HELP1, (0,))
+    stage2(OWN03, (0,))
+    stage1(OWN12, (1,))
+    stage4(HELP1, (1,))
+    stage4(HELP2, (1,))
+    stage2(OWN12, (0,))
+    stage2(OWN03, (1,))
+    help_first()
+    stage2b(OWN03, (0,))
+    stage2(OWN12, (1,))
+    help_last(HELP2)
+    stage2b(OWN12, (0,))
+    stage2b(OWN03, (1,))
+    stage2b(OWN12, (1,))
+    stage3(OWN03, (0,))
+    stage3(OWN03, (1,))
+    stage3(OWN12, (0,))
+    help_last(HELP1)
+    stage3(OWN12, (1,))
+    stage4(OWN03, (0,))
+    stage4(OWN12, (0,))
+    stage4(OWN03, (1,))
+    stage4(OWN12, (1,))
+    own_block(OWN03)
+    own_block(OWN12)
     for role in (0, 3, 1, 2):
         f = freq(role)
         for part in (0, 1):

time: 86.9 us -> 78.2 us (0.90)
  Pallas kernels: 84.5 us -> 75.9 us
    pallas_call x1, Pallas kernels: 84.5 us -> 75.9 us  [shards(): pl.pallas_call(kernel, out_shape=jax.ShapeDtypeStruct((2, F, 256, 128), j...]
where the time goes in v3:
time: 78.2 us; the launch traced here: 78.1 us
  Pallas kernels  75.9 us (97%)
  local copies, waits for them, and re-layouts  2.27 us (3%)
    pallas_call x1, Pallas kernels, shards(): pl.pallas_call(kernel, out_shape=jax.ShapeDtypeStruct((2, F, 256, 128), j...  75.9 us
    unnamed x1, local copies, waits for them, and re-layouts  2.27 us

profile of v3, /device:TPU:1, one launch (start us, length us, event | category | flops | bytes accessed | tf_op | source)
XLA Modules:
  0.0 78.1 jit_solution(696031176592723125)
XLA Ops:
  0.0 75.9 %shard_map.28 = f32[2,4,256,128]{3,2,1,0:T(8,128)} custom-call(bf16[2,4,256,128]{3,2,1,0:T(8,128)(2,1)} %p_ref.1, bf16[2,4,512,128]{3,2,1,0:T(8,128)(2,1)} %d_ref.1), custom_call_target="tpu_custom_call" | custom-call | flops 4294967296 | bytes 3145728 | tf_op jit(solution)/shard_map/pallas_call | solution.py:402
  75.9 2.3 %copy.4 = f32[2,4,256,128]{3,2,1,0:T(8,128)} copy(f32[2,4,256,128]{3,2,1,0:T(8,128)} %shard_map.28) | data formatting | bytes 2097152

commit v4 on v3

--- a/solution.py
+++ b/solution.py
@@ -17,7 +17,7 @@
 
 
 def kernel(
-    p_ref, d_ref, o_ref, pall, dall, cpart, crecv,
+    p_ref, d_ref, own_ref, other_ref, pown, pall, dall, cpart, total,
     stage, help_send, help_recv, stage_send, stage_recv, own_send, own_recv, p_send, p_recv, sib_send, sib_recv, d_send, d_recv, c_send, c_recv, local_sem,
 ):
     z = lax.axis_index("shot")
@@ -40,10 +40,19 @@
     across = (z, rec(0, 2))
     sides = ((z, rec(1, 0)), (z, rec(-1, 0))), ((z, rec(0, 1)), (z, rec(0, -1)))
 
+    own_d = [pltpu.make_async_copy(d_ref.at[:, freq(p)], dall.at[freq(p), p], local_sem.at[p]) for p in range(4)]
+    own_p = pltpu.make_async_copy(p_ref, pown, local_sem.at[4])
+    own_p.start()
+    for copy in own_d:
+        copy.start()
+
     barrier = pltpu.get_barrier_semaphore()
     partners = (sibling, up, down, up2, down2, across) + sides[0] + sides[1]
     for other in partners:
         pl.semaphore_signal(barrier, inc=1, device_id=other, device_id_type=MESH)
+    own_p.wait()
+    for copy in own_d:
+        copy.wait()
     pl.semaphore_wait(barrier, len(partners))
 
     def remote(src, dst, send, recv, device):
@@ -72,7 +81,7 @@
         return away * turned, away * (1 - turned)
 
     def help_copy(role, part, staged):
-        src = stage.at[role, part] if staged else p_ref.at[part, freq(role)]
+        src = stage.at[role, part] if staged else pown.at[part, freq(role)]
         n = 1 if staged else 0
         group = HELP[role]
         return remote(
@@ -81,7 +90,7 @@
 
     def stage_copy(role, part):
         return remote(
-            p_ref.at[part, freq(role)], stage.at[role, part], stage_send.at[role, part], stage_recv.at[role, part], across
+            pown.at[part, freq(role)], stage.at[role, part], stage_send.at[role, part], stage_recv.at[role, part], across
         )
 
     def own_copy(role):
@@ -96,7 +105,7 @@
             dy = is_in((7,), delta) * 3 + is_in((0,), delta) * 2 + is_in((1,), delta)
         group = OWN03 if role in (0, 3) else OWN12
         target = rec_of(x, lax.rem(y + dy, 4), c)
-        src, dst = p_ref.at[:, freq(role)], pall.at[group, :, target]
+        src, dst = pown.at[:, freq(role)], pall.at[group, :, target]
         stays = mine * jnp.where(dy == 0, 1, 0)
         leaves = mine * jnp.where(dy == 0, 0, 1)
 
@@ -161,7 +170,7 @@
 
     def d_copy(role, pos, part, upwards):
         f = freq(role)
-        src = d_ref.at[part, f] if pos == role else dall.at[f, pos, part]
+        src = dall.at[f, pos, part]
         way = 0 if upwards else 1
         return remote(src, dall.at[f, pos, part], d_send.at[way], d_recv.at[f, pos, part], up if upwards else down)
 
@@ -180,10 +189,6 @@
         for part in (0, 1):
             d_copy(i, i, part, True).start()
             d_copy(3 - i, 3 - i, part, False).start()
-
-    own_d = [
-        pltpu.make_async_copy(d_ref.at[:, freq(role)], dall.at[freq(role), role], local_sem.at[role]) for role in range(4)
-    ]
 
     def slot(part, a, b):
         return rec(a, b) if part == 0 else rec(b, a)
@@ -279,32 +284,37 @@
             else:
                 cpart[index, part] += value
 
-    def help_first():
-        for copy in own_d:
-            copy.wait()
-        shared(HELP1).wait_recv()
-        shared(HELP2).wait_recv()
-        for n in range(3):
+    waited = []
+
+    def d_once(role, pos):
+        if (role, pos) not in waited:
+            waited.append((role, pos))
+            d_wait(role, pos)
+
+    def help_first(group, n):
+        if n == 0:
+            shared(group).wait_recv()
+        for role in (0, 3):
             if n > 0:
-                d_wait(0, n)
-                d_wait(3, 3 - n)
-            for group in (HELP2, HELP1):
-                for role in (0, 3):
-                    help_step(group, role, n)
+                d_once(role, n if role == 0 else 3 - n)
+            help_step(group, role, n)
 
     def help_last(group):
         for role in (0, 3):
-            if group == HELP2:
-                d_wait(role, 3 - role)
+            d_once(role, 3 - role)
             help_step(group, role, 3)
             index = (0 if role == 0 else 1) + (0 if group == HELP1 else 2)
             f = freq(role)
             near, far = (down, down2) if role == 0 else (up, up2)
             for part in (0, 1):
                 remote(
-                    cpart.at[index, part], crecv.at[f, part], c_send.at[index], c_recv.at[f, part],
+                    cpart.at[index, part], other_ref.at[part, f], c_send.at[index], c_recv.at[f, part],
                     near if group == HELP1 else far,
                 ).start()
+
+    def out_copy(role):
+        f = freq(role)
+        return pltpu.make_async_copy(total.at[:, f], own_ref.at[:, f], local_sem.at[role])
 
     def own_block(group):
         shared(group).wait_recv()
@@ -313,77 +323,81 @@
             for pos in range(4):
                 for part, value in enumerate(product(group, role, pos)):
                     if pos == 0:
-                        o_ref[part, f] = value
+                        total[part, f] = value
                     else:
-                        o_ref[part, f] += value
+                        total[part, f] += value
+            out_copy(role).start()
 
     place_across()
     place_direct()
     place_own((0, 3))
     place_own((1, 2))
-    for copy in own_d:
-        copy.start()
     d_own(0)
+    stage1(OWN03, (1,))
     stage1(HELP1, (0,))
     place_staged()
+    d_own(1)
     stage1(HELP2, (0,))
+    stage1(OWN12, (0,))
     stage1(OWN03, (0,))
-    d_own(1)
-    stage2(HELP1, (0,))
     stage1(HELP1, (1,))
+    stage1(HELP2, (1,))
     d_own(2)
-    stage1(HELP2, (1,))
     stage2(HELP2, (0,))
-    stage2(HELP1, (1,))
-    stage2b(HELP1, (0,))
-    stage2(HELP2, (1,))
     d_forward(1, 0, True)
     d_forward(2, 3, False)
+    stage2(HELP1, (1,))
+    stage2(HELP2, (1,))
     stage2b(HELP2, (0,))
-    stage2b(HELP1, (1,))
     d_forward(2, 1, True)
     d_forward(1, 2, False)
-    stage3(HELP1, (0,))
+    stage2(HELP1, (0,))
     stage2b(HELP2, (1,))
     stage3(HELP2, (0,))
+    stage2b(HELP1, (1,))
+    stage2b(HELP1, (0,))
+    stage3(HELP2, (1,))
     stage3(HELP1, (1,))
-    stage3(HELP2, (1,))
-    stage1(OWN12, (0,))
+    stage2(OWN03, (1,))
     d_forward(2, 0, True)
     d_forward(1, 3, False)
-    stage1(OWN03, (1,))
+    stage3(HELP1, (0,))
+    stage4(HELP2, (1,))
+    stage1(OWN12, (1,))
+    stage2(OWN03, (0,))
     stage4(HELP2, (0,))
+    stage4(HELP1, (1,))
     stage4(HELP1, (0,))
-    stage2(OWN03, (0,))
-    stage1(OWN12, (1,))
-    stage4(HELP1, (1,))
-    stage4(HELP2, (1,))
+    stage2b(OWN03, (1,))
+    help_first(HELP2, 0)
+    help_first(HELP2, 1)
+    help_first(HELP1, 0)
     stage2(OWN12, (0,))
-    stage2(OWN03, (1,))
-    help_first()
-    stage2b(OWN03, (0,))
+    help_first(HELP1, 1)
+    help_first(HELP1, 2)
+    help_first(HELP2, 2)
     stage2(OWN12, (1,))
     help_last(HELP2)
+    help_last(HELP1)
+    stage2b(OWN03, (0,))
     stage2b(OWN12, (0,))
-    stage2b(OWN03, (1,))
+    stage3(OWN03, (1,))
+    stage3(OWN03, (0,))
     stage2b(OWN12, (1,))
-    stage3(OWN03, (0,))
-    stage3(OWN03, (1,))
     stage3(OWN12, (0,))
-    help_last(HELP1)
     stage3(OWN12, (1,))
+    stage4(OWN03, (1,))
     stage4(OWN03, (0,))
     stage4(OWN12, (0,))
-    stage4(OWN03, (1,))
     stage4(OWN12, (1,))
     own_block(OWN03)
     own_block(OWN12)
     for role in (0, 3, 1, 2):
         f = freq(role)
-        for part in (0, 1):
-            ref = crecv.at[f, part]
+        out_copy(role).wait()
+        for part in (0, 1):
+            ref = other_ref.at[part, f]
             remote(ref, ref, c_send.at[0], c_recv.at[f, part], up).wait_recv()
-            o_ref[part, f] += crecv[f, part]
 
     for index in range(4):
         remote(cpart.at[index], cpart.at[index], c_send.at[index], c_recv.at[0, 0], up).wait_send()
@@ -399,16 +413,17 @@
 
 
 def shards(primaries, recorded):
-    return pl.pallas_call(
+    own, other = pl.pallas_call(
         kernel,
-        out_shape=jax.ShapeDtypeStruct((2, F, 256, 128), jnp.float32),
+        out_shape=(jax.ShapeDtypeStruct((2, F, 256, 128), jnp.float32),) * 2,
         in_specs=[pl.BlockSpec(memory_space=pl.ANY)] * 2,
-        out_specs=pl.BlockSpec(memory_space=pltpu.VMEM),
+        out_specs=(pl.BlockSpec(memory_space=pl.ANY),) * 2,
         scratch_shapes=[
+            pltpu.VMEM((2, F, 256, 128), jnp.bfloat16),
             pltpu.VMEM((4, 2, 2 * NQ, 256, 128), jnp.bfloat16),
             pltpu.VMEM((F, 4, 2, 512, 128), jnp.bfloat16),
             pltpu.VMEM((4, 2, 256, 128), jnp.float32),
-            pltpu.VMEM((F, 2, 256, 128), jnp.float32),
+            pltpu.VMEM((2, F, 256, 128), jnp.float32),
             pltpu.VMEM((4, 2, 256, 128), jnp.bfloat16),
             pltpu.SemaphoreType.DMA((2, 4, 2)),
             pltpu.SemaphoreType.DMA((4, 2)),
@@ -424,13 +439,14 @@
             pltpu.SemaphoreType.DMA((F, 4, 2)),
             pltpu.SemaphoreType.DMA((4,)),
             pltpu.SemaphoreType.DMA((F, 2)),
-            pltpu.SemaphoreType.DMA((4,)),
+            pltpu.SemaphoreType.DMA((5,)),
         ],
         compiler_params=pltpu.CompilerParams(
             collective_id=0, has_side_effects=True, vmem_limit_bytes=56 * 1024 * 1024
         ),
         cost_estimate=pl.CostEstimate(flops=4294967296, bytes_accessed=3 << 20, transcendentals=0),
     )(primaries, recorded)
+    return own + other
 
 
 def solution(mesh):

time: 78.2 us -> 75.8 us (0.969)
  Pallas kernels: 75.9 us -> 73 us
  other arithmetic: 0 us -> 2.62 us
  local copies, waits for them, and re-layouts: 2.27 us -> 0 us
    pallas_call x1, Pallas kernels: 75.9 us -> 73 us  [shards(): pl.pallas_call(kernel, out_shape=(jax.ShapeDtypeStruct((2, F, 256, 128),...]
    add x0 -> x1, other arithmetic: none -> 2.62 us  [shards(): return own + other]
    unnamed x1 -> x0, local copies, waits for them, and re-layouts: 2.27 us -> none
where the time goes in v4:
time: 75.8 us; the launch traced here: 75.7 us
  Pallas kernels  73 us (96%)
  other arithmetic  2.62 us (3%)
    pallas_call x1, Pallas kernels, shards(): pl.pallas_call(kernel, out_shape=(jax.ShapeDtypeStruct((2, F, 256, 128),...  73 us
    add x1, other arithmetic, shards(): return own + other  2.62 us

profile of v4, /device:TPU:1, one launch (start us, length us, event | category | flops | bytes accessed | tf_op | source)
XLA Modules:
  0.0 75.7 jit_solution(2432056835944505505)
XLA Ops:
  0.0 73.0 %shard_map.28 = (f32[2,4,256,128]{3,2,1,0:T(8,128)}, f32[2,4,256,128]{3,2,1,0:T(8,128)}) custom-call(bf16[2,4,256,128]{3,2,1,0:T(8,128)(2,1)} %p_ref.1, bf16[2,4,512,128]{3,2,1,0:T(8,128)(2,1)} %d_ref.1), custom_call_target="tpu_custom_call" | custom-call | flops 4294967296 | bytes 3145728 | tf_op jit(solution)/shard_map/pallas_call | solution.py:416
  73.0 2.6 %add.3 = f32[2,4,256,128]{3,2,1,0:T(8,128)} add(f32[2,4,256,128]{3,2,1,0:T(8,128)} %get-tuple-element.7, f32[2,4,256,128]{3,2,1,0:T(8,128)} %get-tuple-element.8) | non-fusion elementwise | flops 262144 | bytes 3145728 | tf_op jit(solution)/shard_map/add | solution.py:449

commit v5 on v4

--- a/solution.py
+++ b/solution.py
@@ -336,60 +336,60 @@
     stage1(OWN03, (1,))
     stage1(HELP1, (0,))
     place_staged()
+    stage1(OWN03, (0,))
+    stage1(OWN12, (1,))
+    stage1(HELP2, (0,))
     d_own(1)
-    stage1(HELP2, (0,))
-    stage1(OWN12, (0,))
-    stage1(OWN03, (0,))
+    d_own(2)
+    d_forward(1, 0, True)
+    d_forward(2, 3, False)
     stage1(HELP1, (1,))
     stage1(HELP2, (1,))
-    d_own(2)
     stage2(HELP2, (0,))
-    d_forward(1, 0, True)
-    d_forward(2, 3, False)
     stage2(HELP1, (1,))
     stage2(HELP2, (1,))
     stage2b(HELP2, (0,))
+    stage2(HELP1, (0,))
+    stage2b(HELP2, (1,))
     d_forward(2, 1, True)
     d_forward(1, 2, False)
-    stage2(HELP1, (0,))
-    stage2b(HELP2, (1,))
+    stage2b(HELP1, (1,))
     stage3(HELP2, (0,))
-    stage2b(HELP1, (1,))
     stage2b(HELP1, (0,))
     stage3(HELP2, (1,))
     stage3(HELP1, (1,))
-    stage2(OWN03, (1,))
+    stage3(HELP1, (0,))
     d_forward(2, 0, True)
     d_forward(1, 3, False)
-    stage3(HELP1, (0,))
+    stage2(OWN03, (0,))
+    stage2(OWN03, (1,))
+    stage4(HELP2, (0,))
     stage4(HELP2, (1,))
-    stage1(OWN12, (1,))
-    stage2(OWN03, (0,))
-    stage4(HELP2, (0,))
     stage4(HELP1, (1,))
     stage4(HELP1, (0,))
-    stage2b(OWN03, (1,))
+    stage2b(OWN03, (0,))
+    stage1(OWN12, (0,))
     help_first(HELP2, 0)
     help_first(HELP2, 1)
+    stage2(OWN12, (1,))
+    help_first(HELP2, 2)
+    stage3(OWN03, (0,))
+    stage2b(OWN03, (1,))
+    stage2(OWN12, (0,))
+    help_last(HELP2)
     help_first(HELP1, 0)
-    stage2(OWN12, (0,))
     help_first(HELP1, 1)
     help_first(HELP1, 2)
-    help_first(HELP2, 2)
-    stage2(OWN12, (1,))
-    help_last(HELP2)
     help_last(HELP1)
-    stage2b(OWN03, (0,))
+    stage2b(OWN12, (1,))
+    stage3(OWN03, (1,))
     stage2b(OWN12, (0,))
-    stage3(OWN03, (1,))
-    stage3(OWN03, (0,))
-    stage2b(OWN12, (1,))
+    stage3(OWN12, (1,))
     stage3(OWN12, (0,))
-    stage3(OWN12, (1,))
     stage4(OWN03, (1,))
     stage4(OWN03, (0,))
+    stage4(OWN12, (1,))
     stage4(OWN12, (0,))
-    stage4(OWN12, (1,))
     own_block(OWN03)
     own_block(OWN12)
     for role in (0, 3, 1, 2):

time: 75.8 us -> 72.6 us (0.958)
  Pallas kernels: 73 us -> 69.9 us
    pallas_call x1, Pallas kernels: 73 us -> 69.9 us  [shards(): pl.pallas_call(kernel, out_shape=(jax.ShapeDtypeStruct((2, F, 256, 128),...]
where the time goes in v5:
time: 72.6 us; the launch traced here: 72.5 us
  Pallas kernels  69.9 us (96%)
  other arithmetic  2.62 us (4%)
    pallas_call x1, Pallas kernels, shards(): pl.pallas_call(kernel, out_shape=(jax.ShapeDtypeStruct((2, F, 256, 128),...  69.9 us
    add x1, other arithmetic, shards(): return own + other  2.62 us

profile of v5, /device:TPU:1, one launch (start us, length us, event | category | flops | bytes accessed | tf_op | source)
XLA Modules:
  0.0 72.5 jit_solution(10996288131704562555)
XLA Ops:
  0.0 69.9 %shard_map.28 = (f32[2,4,256,128]{3,2,1,0:T(8,128)}, f32[2,4,256,128]{3,2,1,0:T(8,128)}) custom-call(bf16[2,4,256,128]{3,2,1,0:T(8,128)(2,1)} %p_ref.1, bf16[2,4,512,128]{3,2,1,0:T(8,128)(2,1)} %d_ref.1), custom_call_target="tpu_custom_call" | custom-call | flops 4294967296 | bytes 3145728 | tf_op jit(solution)/shard_map/pallas_call | solution.py:416
  69.9 2.6 %add.3 = f32[2,4,256,128]{3,2,1,0:T(8,128)} add(f32[2,4,256,128]{3,2,1,0:T(8,128)} %get-tuple-element.7, f32[2,4,256,128]{3,2,1,0:T(8,128)} %get-tuple-element.8) | non-fusion elementwise | flops 262144 | bytes 3145728 | tf_op jit(solution)/shard_map/add | solution.py:449

commit v6 on v5

--- a/solution.py
+++ b/solution.py
@@ -377,12 +377,12 @@
     stage2b(OWN03, (1,))
     stage2(OWN12, (0,))
     help_last(HELP2)
+    stage2b(OWN12, (1,))
     help_first(HELP1, 0)
     help_first(HELP1, 1)
     help_first(HELP1, 2)
+    stage3(OWN03, (1,))
     help_last(HELP1)
-    stage2b(OWN12, (1,))
-    stage3(OWN03, (1,))
     stage2b(OWN12, (0,))
     stage3(OWN12, (1,))
     stage3(OWN12, (0,))
@@ -392,15 +392,6 @@
     stage4(OWN12, (0,))
     own_block(OWN03)
     own_block(OWN12)
-    for role in (0, 3, 1, 2):
-        f = freq(role)
-        out_copy(role).wait()
-        for part in (0, 1):
-            ref = other_ref.at[part, f]
-            remote(ref, ref, c_send.at[0], c_recv.at[f, part], up).wait_recv()
-
-    for index in range(4):
-        remote(cpart.at[index], cpart.at[index], c_send.at[index], c_recv.at[0, 0], up).wait_send()
     for group in range(4):
         shared(group).wait_send()
         for part in (0, 1):
@@ -410,6 +401,15 @@
         ref = dall.at[pl.ds(0, 3), pl.ds(0, 2)]
         remote(ref, ref, d_send.at[way], d_recv.at[0, 0, 0], up).wait_send()
     place_sent()
+
+    for role in (0, 3, 1, 2):
+        f = freq(role)
+        out_copy(role).wait()
+        for part in (0, 1):
+            ref = other_ref.at[part, f]
+            remote(ref, ref, c_send.at[0], c_recv.at[f, part], up).wait_recv()
+    for index in range(4):
+        remote(cpart.at[index], cpart.at[index], c_send.at[index], c_recv.at[0, 0], up).wait_send()
 
 
 def shards(primaries, recorded):

time: 72.6 us -> 72.5 us (level)
  no operation moved by 1% of the time
where the time goes in v6:
time: 72.5 us; the launch traced here: 72.4 us
  Pallas kernels  69.8 us (96%)
  other arithmetic  2.62 us (4%)
    pallas_call x1, Pallas kernels, shards(): pl.pallas_call(kernel, out_shape=(jax.ShapeDtypeStruct((2, F, 256, 128),...  69.8 us
    add x1, other arithmetic, shards(): return own + other  2.62 us

profile of v6, /device:TPU:1, one launch (start us, length us, event | category | flops | bytes accessed | tf_op | source)
XLA Modules:
  0.0 72.4 jit_solution(16621647032134609265)
XLA Ops:
  0.0 69.8 %shard_map.28 = (f32[2,4,256,128]{3,2,1,0:T(8,128)}, f32[2,4,256,128]{3,2,1,0:T(8,128)}) custom-call(bf16[2,4,256,128]{3,2,1,0:T(8,128)(2,1)} %p_ref.1, bf16[2,4,512,128]{3,2,1,0:T(8,128)(2,1)} %d_ref.1), custom_call_target="tpu_custom_call" | custom-call | flops 4294967296 | bytes 3145728 | tf_op jit(solution)/shard_map/pallas_call | solution.py:416
  69.8 2.6 %add.3 = f32[2,4,256,128]{3,2,1,0:T(8,128)} add(f32[2,4,256,128]{3,2,1,0:T(8,128)} %get-tuple-element.7, f32[2,4,256,128]{3,2,1,0:T(8,128)} %get-tuple-element.8) | non-fusion elementwise | flops 262144 | bytes 3145728 | tf_op jit(solution)/shard_map/add | solution.py:449
